TPU v7x, 32 devices: a whole 2x2x4 slice. The times are simulated.
32 devices in a mesh: groups: 2 (over x), row: 16 (over z, y, core).
Axes of the slice: x: 2, y: 2, z: 4, core: 2. Of those that a mesh axis runs over, the one named last changes fastest.
Arguments:
- active_ids: int32 [256], P(('groups', 'row')), parts along dimension 0, may hold values from 0 to 2047, as said below
- active_layers: int32 [256], P(('groups', 'row')), parts along dimension 0, may hold values from 0 to 15, as said below
- activations: float32 [256], P(('groups', 'row')), parts along dimension 0, may hold values from 0.1 to 10
- kept_tiles: int32 [32, 4], P('groups'), parts along dimension 0, may hold values 0 or 1
- owner_map: int32 [4096], P('groups'), parts along dimension 0, may hold values from 0 to 2047, as said below
- dict_decoder: bfloat16 [4096, 8192], P(('groups', 'row')), parts along dimension 0, may hold values from -0.0625 to 0.0625
- dict_encoder: bfloat16 [4096, 8192], P(('groups', 'row')), parts along dimension 0, may hold values from -6 to 6
Outputs:
- edges: float32 [512, 128], P(('groups', 'row')), parts along dimension 0
- weights: float32 [512, 128], P(('groups', 'row')), parts along dimension 0
There are 2 independent parts, one for each index of `groups`. A program takes and returns all parts, laid end to end along the dimension named above; each array names one. Nothing has to cross between parts.
Inputs may be any that keep to these rules, and one draw needn't show every extreme that they name: `active_ids`: distinct ids; within one device's 8 list entries no two ids share an owner (owner_map value // 128); some owner holds exactly 16 of the 128 ids and none more. `active_layers`: non-decreasing along the list. `owner_map`: a permutation: slot s is stored on row device s // 128.
All inputs are finite; a program needn't handle non-finite values.
Results may differ from a plain program's by a relative error of at most 0.0003.
Values may be sent and summed in bfloat16 or wider, within the bound.
A program may use at most 64 MiB of HBM per device.

v0:
```python
import jax
import jax.numpy as jnp
from jax import lax
from jax.sharding import PartitionSpec as P


def contract(left, right):
    return lax.dot_general(
        left, right, (((1,), (1,)), ((), ())), preferred_element_type=jnp.float32
    )


def shards(
    active_ids, active_layers, activations, kept_tiles, owner_map, dict_decoder, dict_encoder
):
    devices = lax.axis_size("row")
    myself = lax.axis_index("row")
    tile_rows = active_ids.shape[0]
    stored = dict_decoder.shape[0]
    capacity = 2 * tile_rows
    roster_ids, roster_layers = (
        lax.all_gather(active_ids, "row", axis=0, tiled=True),
        lax.all_gather(active_layers, "row", axis=0, tiled=True),
    )
    roster_acts = lax.all_gather(activations, "row", axis=0, tiled=True)
    features = roster_ids.shape[0]
    storage = jnp.take(owner_map, roster_ids)
    owners = storage // stored
    local_rows = storage % stored
    onehot = (owners[:, None] == jnp.arange(devices, dtype=jnp.int32)[None, :]).astype(jnp.int32)
    places = jnp.sum((jnp.cumsum(onehot, axis=0) - onehot) * onehot, axis=1)
    owned = owners == myself
    positions = jnp.arange(features, dtype=jnp.int32)
    chosen = (
        owned[None, :] & (places[None, :] == jnp.arange(capacity, dtype=jnp.int32)[:, None])
    ).astype(jnp.int32)
    filled = jnp.sum(chosen, axis=1) > 0
    row_index = jnp.sum(chosen * positions[None, :], axis=1)
    row_local = jnp.sum(chosen * local_rows[None, :], axis=1)
    row_layer = jnp.take(roster_layers, row_index)
    row_act = jnp.take(roster_acts, row_index)
    sources = jnp.take(dict_decoder, row_local, axis=0)
    column_index = owners * capacity + places
    packed = jnp.where(
        filled[:, None],
        jnp.take(dict_encoder, row_local, axis=0),
        jnp.zeros((), dict_encoder.dtype),
    )
    packed_scores = contract(sources, lax.all_gather(packed, "row", axis=0, tiled=True))
    dots = jnp.take(packed_scores, column_index, axis=1)
    kept_rows = jnp.take(kept_tiles, row_index // tile_rows, axis=0)
    kept_columns = jnp.repeat(
        kept_rows, features // kept_tiles.shape[1], axis=1, total_repeat_length=features
    )
    allowed = filled[:, None] & (row_layer[:, None] < roster_layers[None, :]) & (kept_columns > 0)
    edges = jnp.where(allowed, row_act[:, None] * dots, jnp.float32(0))
    magnitude = jnp.abs(edges)
    column_total, column_count = lax.psum(
        (jnp.sum(magnitude, axis=0), jnp.sum(allowed.astype(jnp.float32), axis=0)), "row"
    )
    weights = magnitude * jnp.maximum(column_count, 1.0) / jnp.maximum(column_total, 1.0)
    return (edges, weights)


def solution(mesh):
    in_specs = (
        P(("groups", "row")),
        P(("groups", "row")),
        P(("groups", "row")),
        P("groups", None),
        P("groups"),
        P(("groups", "row"), None),
        P(("groups", "row"), None),
    )
    out_specs = (P(("groups", "row"), None), P(("groups", "row"), None))
    return jax.shard_map(shards, mesh=mesh, in_specs=in_specs, out_specs=out_specs, check_vma=False)
```

profile of v0, /device:TPU:0, one launch (start us, length us, event | category | flops | bytes accessed | tf_op | source)
XLA Modules:
  0.0 120.7 jit_solution(11442184285242747412)
XLA Ops:
  7.3 1.4 %dynamic-slice.6 = u32[1]{0:T(128)} dynamic-slice(u32[32]{0:T(128)} %constant.221, u32[]{:T(128)S(6)} %add.125), dynamic_slice_sizes={1} | dynamic-slice | bytes 12
  9.3 0.9 dynamic-update-slice.3
  10.2 0.8 dynamic-update-slice.4
  11.0 13.7 %all-reduce.3 = (s32[128]{0:T(128)S(1)}, s32[128]{0:T(128)S(1)}) all-reduce(s32[128]{0:T(128)S(1)} %dynamic-update-slice.3, s32[128]{0:T(128)S(1)} %dynamic-update-slice.4), channel_id=1, replica_groups=mesh['groups'=2,'row'=16] {'row'}, use_global_device_ids=true, to_apply=%add | all-reduce | flops 256 | bytes 2048
  24.7 1.6 %gather_fusion = s32[128]{0:T(128)S(1)} fusion(s32[2048]{0:T(1024)} %param.15, s32[1024]{0:T(1024)S(1)} %pad_clamp_fusion.5), kind=kCustom, calls=%fused_computation.2 | custom fusion | bytes 1536 | tf_op jit(solution)/shard_map/jit(_take)/gather | solution.py:27
  26.5 0.2 reduce_window_sum.22
  26.7 0.2 select_reduce_fusion
  27.0 0.7 gather_fusion.7
  27.8 0.8 select_select_fusion
  28.6 2.8 %gather_fusion.6 = bf16[16,8192]{1,0:T(8,128)(2,1)S(1)} fusion(bf16[128,8192]{1,0:T(8,128)(2,1)} %param.16, s32[1024]{0:T(1024)S(1)} %pad_clamp_fusion.1), kind=kCustom, calls=%fused_computation.clone | custom fusion | bytes 524352 | tf_op jit(solution)/shard_map/jit(_take)/gather | solution.py:42
  31.4 0.2 dynamic-update-slice.5
  31.6 30.1 %all-reduce.2 = f32[128]{0:T(128)S(1)} all-reduce(f32[128]{0:T(128)S(1)} %dynamic-update-slice.5), channel_id=1, replica_groups=mesh['groups'=2,'row'=16] {'row'}, use_global_device_ids=true, to_apply=%add.2 | all-reduce | flops 128 | bytes 1024
  61.7 0.7 gather_fusion.4
  62.4 0.7 gather_fusion.1
  63.2 0.6 gather_fusion.2
  63.9 0.6 gather_fusion.3
  64.6 0.2 convert_reduce_fusion
  64.8 12.1 %all-gather.2.cloned.1.call-done = bf16[256,8192]{1,0:T(8,128)(2,1)} async-done(((bf16[16,8192]{1,0:T(8,128)(2,1)}), bf16[256,8192]{1,0:T(8,128)(2,1)}) %all-gather.2.cloned.1.call-update) | async-done | bytes 4194320 | tf_op jit(solution)/shard_map/all_gather | solution.py:49
  76.9 3.5 %fusion = f32[16,256]{0,1:T(8,128)S(1)} fusion(bf16[256,8192]{1,0:T(8,128)(2,1)} %all-gather.2.cloned.1.call-done, bf16[16,8192]{1,0:T(8,128)(2,1)S(1)} %gather_fusion.6, pred[16]{0:T(512)(128)(4,1)S(1)} %get-tuple-element.39), kind=kOutput, calls=%fused_computation.9 | convolution fusion | flops 67239936 | bytes 4472848 | tf_op jit(solution)/shard_map/dot_general | solution.py:8
  80.4 0.6 gather_fusion.5
  81.0 0.2 abs_reduce_fusion
  81.2 31.3 %all-reduce.4 = (f32[128]{0:T(128)S(1)}, f32[128]{0:T(128)S(1)}) all-reduce(f32[128]{0:T(128)S(1)} %get-tuple-element.30, f32[128]{0:T(128)S(1)} %get-tuple-element.28), channel_id=1, replica_groups=mesh['groups'=2,'row'=16] {'row'}, use_global_device_ids=true, to_apply=%region_8.10 | all-reduce | flops 256 | bytes 2048 | tf_op jit(solution)/shard_map/psum | solution.py:58
  112.5 0.7 copy.22
  113.2 0.7 copy.23
  (37 shorter events, 0.8 us)
Async XLA Ops:
  7.2 19.9 %copy-start = (bf16[128,8192]{1,0:T(8,128)(2,1)S(1)}, bf16[128,8192]{1,0:T(8,128)(2,1)}, u32[]{:S(2)}) copy-start(bf16[128,8192]{1,0:T(8,128)(2,1)} %param.17) | copy-start | bytes 6291460
  7.2 56.7 %copy-start.2 = (s32[128]{0:T(128)S(1)}, s32[128]{0:T(128)}, u32[]{:S(2)}) copy-start(s32[128]{0:T(128)} %constant.218) | copy-start | bytes 1540
  7.2 24.2 %copy-start.3 = (f32[8]{0:T(128)S(1)}, f32[8]{0:T(128)}, u32[]{:S(2)}) copy-start(f32[8]{0:T(128)} %param.13) | copy-start | bytes 100
  7.2 55.9 %copy-start.1 = (s32[16,4]{0,1:T(4,128)S(1)}, s32[16,4]{0,1:T(4,128)}, u32[]{:S(2)}) copy-start(s32[16,4]{0,1:T(4,128)} %param.14) | copy-start | bytes 772
  7.2 69.7 %all-gather.2.cloned.1.call-start = ((), (), s32[]{:S(2)}) async-start(), calls=%async_computation | async-start | bytes 4456448 | tf_op jit(solution)/shard_map/all_gather | solution.py:49
Sparse Core Ops, SparseCore 0:
  28.7 48.1 all-gather.1
where the time goes:
time: 121 us
  blocking collectives  75.1 us (62%)
  between operations  14.9 us (12%)
  local copies, waits for them, and re-layouts  13.2 us (11%)
  waiting for transfers between devices  12.1 us (10%)
  matrix products  3.48 us (3%)
  other arithmetic  2.02 us (2%)
    unnamed x2, blocking collectives  43.8 us
    psum x1, blocking collectives, shards(): lax.psum((jnp.sum(magnitude, axis=0), jnp.sum(allowed.astype(jnp.float32)...  31.3 us
    all_gather x1, waiting for transfers between devices, shards(): lax.all_gather(packed, 'row', axis=0, tiled=True)  12.1 us
    unnamed x18, local copies, waits for them, and re-layouts  4.76 us
    dot_general x1, matrix products, contract(): lax.dot_general(left, right, (((1,), (1,)), ((), ())), preferred_element_...  3.48 us
    gather x1, local copies, waits for them, and re-layouts, shards(): sources = jnp.take(dict_decoder, row_local, axis=0)  2.81 us
  transfers between devices with their start and end apart: 1, of which 1 were waited for; matrix products, arithmetic and copies ran while one was open for 5% of the time, Pallas kernels for 0%

commit v1 on v0

v1 whole, which is shorter than its diff:
```python
import functools

import jax
import jax.numpy as jnp
from jax import lax
from jax.experimental import pallas as pl
from jax.experimental.pallas import tpu as pltpu
from jax.sharding import PartitionSpec as P

MESH = pl.DeviceIdType.MESH


def far_first(n):
    return sorted(range(1, n), key=lambda m: abs(2 * m - n))


def iota(shape, axis):
    return lax.broadcasted_iota(jnp.int32, shape, axis)


def kernel(
    n,
    ids_ref,
    layers_ref,
    acts_ref,
    map_ref,
    kept_ref,
    dec_ref,
    enc_ref,
    edges_ref,
    weights_ref,
    stored_vm,
    meta_out,
    meta_in,
    rows_out,
    rows_in,
    part_out,
    part_in,
    total_out,
    total_in,
    load_sem,
    send_sem,
    recv_sem,
):
    me = lax.axis_index("row")
    mine = ids_ref.shape[0]
    stored, width = dec_ref.shape
    feats = n * mine
    cap = 2 * mine
    chunk = width // n
    offsets = far_first(n)

    loads = [
        pltpu.make_async_copy(dec_ref, stored_vm.at[pl.ds(0, stored)], load_sem.at[0]),
        pltpu.make_async_copy(enc_ref, stored_vm.at[pl.ds(stored, stored)], load_sem.at[1]),
    ]
    for load in loads:
        load.start()

    barrier = pltpu.get_barrier_semaphore()
    for m in offsets:
        pl.semaphore_signal(
            barrier, inc=1, device_id={"row": lax.rem(me + m, n)}, device_id_type=MESH
        )

    lane = iota((8, feats), 1)
    field = iota((8, feats), 0)
    block = jnp.zeros((8, feats), jnp.float32)
    for k in range(mine):
        slot = map_ref[ids_ref[k]]
        here = lane == me * mine + k
        whole = jnp.where(
            field == 0, slot // stored, jnp.where(field == 1, slot % stored, layers_ref[k])
        ).astype(jnp.float32)
        block = jnp.where(here, jnp.where(field == 3, acts_ref[k], whole), block)
    meta_out[...] = block
    meta_in[me] = block

    pl.semaphore_wait(barrier, n - 1)

    def exchange(phase, source, target):
        copies = []
        for m in offsets:
            copy = pltpu.make_async_remote_copy(
                src_ref=source(lax.rem(me + m, n)),
                dst_ref=target,
                send_sem=send_sem.at[phase, m],
                recv_sem=recv_sem.at[phase, m],
                device_id={"row": lax.rem(me + m, n)},
                device_id_type=MESH,
            )
            copy.start()
            copies.append(copy)
        return copies

    first = exchange(0, lambda p: meta_out, meta_in.at[me])
    before = (iota((feats, feats), 0) < iota((feats, feats), 1)).astype(jnp.bfloat16)
    for copy in first:
        copy.wait_recv()
    meta = jnp.sum(meta_in[...], axis=0)
    owner = meta[0:1].astype(jnp.int32)
    local = meta[1:2].astype(jnp.int32)
    layer = meta[2:3]
    act = meta[3:4]
    by_owner = (jnp.broadcast_to(owner, (n, feats)) == iota((n, feats), 0)).astype(jnp.float32)
    earlier = jnp.dot(by_owner.astype(jnp.bfloat16), before, preferred_element_type=jnp.float32)
    place = jnp.sum(by_owner * earlier, axis=0, keepdims=True).astype(jnp.int32)
    packed = jnp.where(owner == me, place, -1)
    chosen = jnp.broadcast_to(packed, (cap, feats)) == iota((cap, feats), 0)
    pick = jnp.sum(
        jnp.where(chosen, jnp.broadcast_to(local + 1, (cap, feats)).astype(jnp.float32), 0.0),
        axis=1,
        keepdims=True,
    )
    pick = jnp.concatenate([pick, pick], axis=0)
    column = iota((2 * cap, 2 * stored), 1)
    second = iota((2 * cap, 2 * stored), 0) >= cap
    sought = jnp.where(second, column - stored, column) + 1
    sought = jnp.where(sought <= 0, -1, jnp.where(sought > stored, -1, sought))
    select = (
        jnp.broadcast_to(pick, (2 * cap, 2 * stored)) == sought.astype(jnp.float32)
    ).astype(jnp.bfloat16)

    for load in loads:
        load.wait()

    def selected(p):
        return jnp.dot(
            select,
            stored_vm[:, pl.ds(pl.multiple_of(p * chunk, chunk), chunk)],
            preferred_element_type=jnp.float32,
        ).astype(jnp.bfloat16)

    def take_and_give(p):
        rows_out[p] = selected(p)
        return rows_out.at[p]

    bulk = exchange(1, take_and_give, rows_in.at[me])
    rows_in[me] = selected(me)

    kept = kept_ref[...]
    tiles, column_tiles = kept.shape
    spread = jnp.zeros((tiles, feats), jnp.int32)
    for c in range(column_tiles):
        within = iota((tiles, feats), 1) // (feats // column_tiles) == c
        spread = jnp.where(within, jnp.broadcast_to(kept[:, c : c + 1], (tiles, feats)), spread)
    spread = jnp.broadcast_to(spread[:, None, :], (tiles, mine, feats)).reshape(feats, feats)
    layer_down = jnp.transpose(jnp.broadcast_to(layer, (feats, feats)))
    allowed = jnp.where(
        layer_down < jnp.broadcast_to(layer, (feats, feats)),
        jnp.where(spread > 0, 1.0, 0.0),
        0.0,
    )
    count = jnp.sum(allowed, axis=0, keepdims=True)
    chosen_f = jnp.where(chosen, 1.0, 0.0)
    allowed_mine = jnp.dot(
        chosen_f.astype(jnp.bfloat16),
        allowed.astype(jnp.bfloat16),
        preferred_element_type=jnp.float32,
    )
    act_mine = jnp.sum(chosen_f * act, axis=1, keepdims=True)
    place_of = owner * cap + place
    position = (
        jnp.broadcast_to(place_of, (n * cap, feats)) == iota((n * cap, feats), 0)
    ).astype(jnp.float32)
    ordering = jnp.transpose(position).astype(jnp.bfloat16)

    for copy in bulk:
        copy.wait_recv()
    sources = rows_in[:, :cap, :].reshape(n * cap, chunk)
    targets = rows_in[:, cap:, :].reshape(n * cap, chunk)
    targets = jnp.dot(ordering, targets, preferred_element_type=jnp.float32).astype(jnp.bfloat16)
    part = lax.dot_general(
        sources, targets, (((1,), (1,)), ((), ())), preferred_element_type=jnp.float32
    )
    part_out[...] = part.reshape(n, cap, feats)
    sums = exchange(2, lambda p: part_out.at[p], part_in.at[me])
    part_in[me] = part_out[me]
    for copy in sums:
        copy.wait_recv()
    dots = jnp.sum(part_in[...], axis=0)
    edges = jnp.where(allowed_mine > 0.0, act_mine * dots, 0.0)
    edges_ref[...] = edges
    magnitude = jnp.abs(edges)
    partial = jnp.sum(magnitude.reshape(cap // 8, 8, feats), axis=0)
    total_out[...] = partial
    total_in[me] = partial
    totals = exchange(3, lambda p: total_out, total_in.at[me])
    for copy in totals:
        copy.wait_recv()
    total = jnp.sum(jnp.sum(total_in[...], axis=0), axis=0, keepdims=True)
    weights_ref[...] = magnitude * jnp.maximum(count, 1.0) / jnp.maximum(total, 1.0)
    for copy in first + bulk + sums + totals:
        copy.wait_send()


def solution(mesh):
    n = mesh.shape["row"]

    def shards(ids, layers, acts, kept, owner_map, decoder, encoder):
        mine = ids.shape[0]
        stored, width = decoder.shape
        feats, cap = n * mine, 2 * mine
        smem = pl.BlockSpec(memory_space=pltpu.SMEM)
        vmem = pl.BlockSpec(memory_space=pltpu.VMEM)
        hbm = pl.BlockSpec(memory_space=pl.ANY)
        result = jax.ShapeDtypeStruct((cap, feats), jnp.float32)
        return pl.pallas_call(
            functools.partial(kernel, n),
            out_shape=(result, result),
            in_specs=[smem, smem, smem, smem, vmem, hbm, hbm],
            out_specs=(vmem, vmem),
            scratch_shapes=[
                pltpu.VMEM((2 * stored, width), decoder.dtype),
                pltpu.VMEM((8, feats), jnp.float32),
                pltpu.VMEM((n, 8, feats), jnp.float32),
                pltpu.VMEM((n, 2 * cap, width // n), decoder.dtype),
                pltpu.VMEM((n, 2 * cap, width // n), decoder.dtype),
                pltpu.VMEM((n, cap, feats), jnp.float32),
                pltpu.VMEM((n, cap, feats), jnp.float32),
                pltpu.VMEM((8, feats), jnp.float32),
                pltpu.VMEM((n, 8, feats), jnp.float32),
                pltpu.SemaphoreType.DMA((2,)),
                pltpu.SemaphoreType.DMA((4, n)),
                pltpu.SemaphoreType.DMA((4, n)),
            ],
            compiler_params=pltpu.CompilerParams(
                collective_id=0, has_side_effects=True, vmem_limit_bytes=40 * 1024 * 1024
            ),
        )(ids, layers, acts, owner_map, kept, decoder, encoder)

    split = P(("groups", "row"))
    wide = P(("groups", "row"), None)
    return jax.shard_map(
        shards,
        mesh=mesh,
        in_specs=(split, split, split, P("groups", None), P("groups"), wide, wide),
        out_specs=(wide, wide),
        check_vma=False,
    )
```

time: 121 us -> 43.4 us (0.36)
  blocking collectives: 75.1 us -> 0 us
  Pallas kernels: 0 us -> 34.7 us
  between operations: 14.9 us -> 0.64 us
  waiting for transfers between devices: 12.1 us -> 0 us
  local copies, waits for them, and re-layouts: 13.2 us -> 7.8 us
  matrix products: 3.48 us -> 0 us
  other arithmetic: 2.02 us -> 0 us
    unnamed x2 -> x0, blocking collectives: 43.8 us -> none
    pallas_call x0 -> x1, Pallas kernels: none -> 34.7 us  [shards(): pl.pallas_call(functools.partial(kernel, n), out_shape=(result, result),...]
    psum x1 -> x0, blocking collectives: 31.3 us -> none  [shards(): lax.psum((jnp.sum(magnitude, axis=0), jnp.sum(allowed.astype(jnp.float32)...]
    all_gather x1 -> x0, waiting for transfers between devices: 12.1 us -> none  [shards(): lax.all_gather(packed, 'row', axis=0, tiled=True)]
    gather x8 -> x0, local copies, waits for them, and re-layouts: 8.32 us -> none  [the longest x1 2.81 us: shards(): sources = jnp.take(dict_decoder, row_local, axis=0)]
    dot_general x1 -> x0, matrix products: 3.48 us -> none  [contract(): lax.dot_general(left, right, (((1,), (1,)), ((), ())), preferred_element_...]
    unnamed x18 -> x15, local copies, waits for them, and re-layouts: 4.76 us -> 7.8 us
  transfers between devices with their start and end apart: 1 -> 0, of which waited for: 1 -> 0; matrix products, arithmetic and copies ran while one was open for 5% -> 0% of each run, Pallas kernels for 0% -> 0%
where the time goes in v1:
time: 43.4 us; the launch traced here: 43.2 us
  Pallas kernels  34.7 us (80%)
  local copies, waits for them, and re-layouts  7.8 us (18%)
  between operations  0.64 us (1%)
    pallas_call x1, Pallas kernels, shards(): pl.pallas_call(functools.partial(kernel, n), out_shape=(result, result),...  34.7 us
    unnamed x15, local copies, waits for them, and re-layouts  7.8 us

profile of v1, /device:TPU:0, one launch (start us, length us, event | category | flops | bytes accessed | tf_op | source)
XLA Modules:
  0.0 43.2 jit_solution(12574411816727511224)
XLA Ops:
  0.6 0.8 %copy.9.kept_ref = s32[16,4]{1,0:T(8,128)S(1)} copy(s32[16,4]{0,1:T(4,128)} %param.10) | data formatting | bytes 512 | tf_op args[3]
  1.4 0.0 copy-start
  1.4 1.6 %copy-done = bf16[128,8192]{1,0:T(8,128)(2,1)S(1)} copy-done((bf16[128,8192]{1,0:T(8,128)(2,1)S(1)}, bf16[128,8192]{1,0:T(8,128)(2,1)}, u32[]{:S(2)}) %copy-start) | copy-done | bytes 2097176
  3.0 0.0 copy-start.1
  3.0 1.6 %copy-done.1 = bf16[128,8192]{1,0:T(8,128)(2,1)S(1)} copy-done((bf16[128,8192]{1,0:T(8,128)(2,1)S(1)}, bf16[128,8192]{1,0:T(8,128)(2,1)}, u32[]{:S(2)}) %copy-start.1) | copy-done | bytes 2097176
  4.6 0.0 copy-start.2
  4.6 0.7 %copy-done.2 = s32[2048]{0:T(1024)S(1)} copy-done((s32[2048]{0:T(1024)S(1)}, s32[2048]{0:T(1024)}, u32[]{:S(2)}) %copy-start.2) | copy-done | bytes 8216
  5.3 0.0 copy-start.3
  5.3 0.7 %copy-done.3 = s32[8]{0:T(128)S(1)} copy-done((s32[8]{0:T(128)S(1)}, s32[8]{0:T(128)}, u32[]{:S(2)}) %copy-start.3) | copy-done | bytes 56
  5.9 0.0 copy-start.4
  5.9 0.7 %copy-done.4 = s32[8]{0:T(128)S(1)} copy-done((s32[8]{0:T(128)S(1)}, s32[8]{0:T(128)}, u32[]{:S(2)}) %copy-start.4) | copy-done | bytes 56
  6.6 0.0 copy-start.5
  6.6 0.7 %copy-done.5 = f32[8]{0:T(128)S(1)} copy-done((f32[8]{0:T(128)S(1)}, f32[8]{0:T(128)}, u32[]{:S(2)}) %copy-start.5) | copy-done | bytes 56
  7.2 34.7 %shard_map.86 = (f32[16,128]{1,0:T(8,128)S(1)}, f32[16,128]{1,0:T(8,128)S(1)}) custom-call(s32[8]{0:T(128)S(1)} %copy-done.3, s32[8]{0:T(128)S(1)} %copy-done.4, f32[8]{0:T(128)S(1)} %copy-done.5, s32[2048]{0:T(1024)S(1)} %copy-done.2, s32[16,4]{1,0:T(8,128)S(1)} %copy.9.kept_ref, bf16[128,8192]{1,0:T(8,128)(2,1)S(1)} %copy-done, bf16[128,8192]{1,0:T(8,128)(2,1)S(1)} %copy-done.1), custom_call_target="tpu_custom_call" | custom-call | tf_op jit(solution)/shard_map/pallas_call | solution.py:208
  42.0 0.6 %copy.12 = f32[16,128]{1,0:T(8,128)} copy(f32[16,128]{1,0:T(8,128)S(1)} %get-tuple-element.4) | data formatting | bytes 16384
  42.6 0.6 %copy.13 = f32[16,128]{1,0:T(8,128)} copy(f32[16,128]{1,0:T(8,128)S(1)} %get-tuple-element.5) | data formatting | bytes 16384
Async XLA Ops:
  1.4 1.6 %copy-start = (bf16[128,8192]{1,0:T(8,128)(2,1)S(1)}, bf16[128,8192]{1,0:T(8,128)(2,1)}, u32[]{:S(2)}) copy-start(bf16[128,8192]{1,0:T(8,128)(2,1)} %dec_ref.1) | copy-start | bytes 6291460
  3.0 1.6 %copy-start.1 = (bf16[128,8192]{1,0:T(8,128)(2,1)S(1)}, bf16[128,8192]{1,0:T(8,128)(2,1)}, u32[]{:S(2)}) copy-start(bf16[128,8192]{1,0:T(8,128)(2,1)} %enc_ref.1) | copy-start | bytes 6291460
  4.6 0.7 %copy-start.2 = (s32[2048]{0:T(1024)S(1)}, s32[2048]{0:T(1024)}, u32[]{:S(2)}) copy-start(s32[2048]{0:T(1024)} %map_ref.1) | copy-start | bytes 24580
  5.3 0.7 %copy-start.3 = (s32[8]{0:T(128)S(1)}, s32[8]{0:T(128)}, u32[]{:S(2)}) copy-start(s32[8]{0:T(128)} %ids_ref.1) | copy-start | bytes 100
  5.9 0.7 %copy-start.4 = (s32[8]{0:T(128)S(1)}, s32[8]{0:T(128)}, u32[]{:S(2)}) copy-start(s32[8]{0:T(128)} %layers_ref.1) | copy-start | bytes 100
  6.6 0.7 %copy-start.5 = (f32[8]{0:T(128)S(1)}, f32[8]{0:T(128)}, u32[]{:S(2)}) copy-start(f32[8]{0:T(128)} %acts_ref.1) | copy-start | bytes 100

commit v2 on v1

--- a/solution.py
+++ b/solution.py
@@ -10,8 +10,19 @@
 MESH = pl.DeviceIdType.MESH
 
 
+def partner(me, m, n):
+    if n & (n - 1):
+        return lax.rem(me + m, n)
+    other, digit = me, 1
+    while digit < n:
+        if m & digit:
+            other = other + digit - 2 * digit * lax.rem(me // digit, 2)
+        digit *= 2
+    return other
+
+
 def far_first(n):
-    return sorted(range(1, n), key=lambda m: abs(2 * m - n))
+    return list(range(n // 2, n)) + list(range(n // 2 - 1, 0, -1))
 
 
 def iota(shape, axis):
@@ -20,15 +31,19 @@
 
 def kernel(
     n,
-    ids_ref,
-    layers_ref,
-    acts_ref,
-    map_ref,
+    ids_hbm,
+    layers_hbm,
+    acts_hbm,
+    map_hbm,
     kept_ref,
     dec_ref,
     enc_ref,
     edges_ref,
     weights_ref,
+    ids_ref,
+    layers_ref,
+    acts_ref,
+    map_ref,
     stored_vm,
     meta_out,
     meta_in,
@@ -54,18 +69,26 @@
         pltpu.make_async_copy(dec_ref, stored_vm.at[pl.ds(0, stored)], load_sem.at[0]),
         pltpu.make_async_copy(enc_ref, stored_vm.at[pl.ds(stored, stored)], load_sem.at[1]),
     ]
-    for load in loads:
+    small = [
+        pltpu.make_async_copy(source, target, load_sem.at[2 + i])
+        for i, (source, target) in enumerate(
+            [(ids_hbm, ids_ref), (map_hbm, map_ref), (layers_hbm, layers_ref), (acts_hbm, acts_ref)]
+        )
+    ]
+    for load in small + loads:
         load.start()
 
     barrier = pltpu.get_barrier_semaphore()
     for m in offsets:
         pl.semaphore_signal(
-            barrier, inc=1, device_id={"row": lax.rem(me + m, n)}, device_id_type=MESH
+            barrier, inc=1, device_id={"row": partner(me, m, n)}, device_id_type=MESH
         )
 
     lane = iota((8, feats), 1)
     field = iota((8, feats), 0)
     block = jnp.zeros((8, feats), jnp.float32)
+    for load in small:
+        load.wait()
     for k in range(mine):
         slot = map_ref[ids_ref[k]]
         here = lane == me * mine + k
@@ -82,11 +105,11 @@
         copies = []
         for m in offsets:
             copy = pltpu.make_async_remote_copy(
-                src_ref=source(lax.rem(me + m, n)),
+                src_ref=source(partner(me, m, n)),
                 dst_ref=target,
                 send_sem=send_sem.at[phase, m],
                 recv_sem=recv_sem.at[phase, m],
-                device_id={"row": lax.rem(me + m, n)},
+                device_id={"row": partner(me, m, n)},
                 device_id_type=MESH,
             )
             copy.start()
@@ -138,8 +161,8 @@
     bulk = exchange(1, take_and_give, rows_in.at[me])
     rows_in[me] = selected(me)
 
-    kept = kept_ref[...]
-    tiles, column_tiles = kept.shape
+    column_tiles, tiles = kept_ref.shape
+    kept = jnp.transpose(kept_ref[...])
     spread = jnp.zeros((tiles, feats), jnp.int32)
     for c in range(column_tiles):
         within = iota((tiles, feats), 1) // (feats // column_tiles) == c
@@ -201,16 +224,19 @@
         mine = ids.shape[0]
         stored, width = decoder.shape
         feats, cap = n * mine, 2 * mine
-        smem = pl.BlockSpec(memory_space=pltpu.SMEM)
         vmem = pl.BlockSpec(memory_space=pltpu.VMEM)
-        hbm = pl.BlockSpec(memory_space=pl.ANY)
+        hbm = pl.BlockSpec(memory_space=pltpu.HBM)
         result = jax.ShapeDtypeStruct((cap, feats), jnp.float32)
         return pl.pallas_call(
             functools.partial(kernel, n),
             out_shape=(result, result),
-            in_specs=[smem, smem, smem, smem, vmem, hbm, hbm],
+            in_specs=[hbm, hbm, hbm, hbm, vmem, hbm, hbm],
             out_specs=(vmem, vmem),
             scratch_shapes=[
+                pltpu.SMEM(ids.shape, jnp.int32),
+                pltpu.SMEM(layers.shape, jnp.int32),
+                pltpu.SMEM(acts.shape, jnp.float32),
+                pltpu.SMEM(owner_map.shape, jnp.int32),
                 pltpu.VMEM((2 * stored, width), decoder.dtype),
                 pltpu.VMEM((8, feats), jnp.float32),
                 pltpu.VMEM((n, 8, feats), jnp.float32),
@@ -220,14 +246,14 @@
                 pltpu.VMEM((n, cap, feats), jnp.float32),
                 pltpu.VMEM((8, feats), jnp.float32),
                 pltpu.VMEM((n, 8, feats), jnp.float32),
-                pltpu.SemaphoreType.DMA((2,)),
+                pltpu.SemaphoreType.DMA((6,)),
                 pltpu.SemaphoreType.DMA((4, n)),
                 pltpu.SemaphoreType.DMA((4, n)),
             ],
             compiler_params=pltpu.CompilerParams(
-                collective_id=0, has_side_effects=True, vmem_limit_bytes=40 * 1024 * 1024
+                collective_id=0, has_side_effects=True, vmem_limit_bytes=64 * 1024 * 1024
             ),
-        )(ids, layers, acts, owner_map, kept, decoder, encoder)
+        )(ids, layers, acts, owner_map, kept.T, decoder, encoder)
 
     split = P(("groups", "row"))
     wide = P(("groups", "row"), None)

time: 43.4 us -> 38.2 us (0.88)
  local copies, waits for them, and re-layouts: 7.8 us -> 2.59 us
    unnamed x15 -> x2, local copies, waits for them, and re-layouts: 7.8 us -> 2.59 us
where the time goes in v2:
time: 38.2 us; the launch traced here: 37.8 us
  Pallas kernels  34.6 us (91%)
  local copies, waits for them, and re-layouts  2.59 us (7%)
  between operations  0.64 us (2%)
    pallas_call x1, Pallas kernels, shards(): pl.pallas_call(functools.partial(kernel, n), out_shape=(result, result),...  34.6 us
    unnamed x2, local copies, waits for them, and re-layouts  2.59 us

profile of v2, /device:TPU:0, one launch (start us, length us, event | category | flops | bytes accessed | tf_op | source)
XLA Modules:
  0.0 37.8 jit_solution(18405649079525743964)
XLA Ops:
  0.6 34.6 %shard_map.86 = (f32[16,128]{1,0:T(8,128)}, f32[16,128]{1,0:T(8,128)}) custom-call(s32[8]{0:T(128)} %ids_hbm.1, s32[8]{0:T(128)} %layers_hbm.1, f32[8]{0:T(128)} %acts_hbm.1, s32[2048]{0:T(1024)} %map_hbm.1, s32[4,16]{1,0:T(4,128)} %bitcast.1, bf16[128,8192]{1,0:T(8,128)(2,1)} %dec_ref.1, bf16[128,8192]{1,0:T(8,128)(2,1)} %enc_ref.1), custom_call_target="tpu_custom_call" | custom-call | tf_op jit(solution)/shard_map/pallas_call | solution.py:230
  35.3 1.3 %copy.11 = f32[16,128]{1,0:T(8,128)} copy(f32[16,128]{1,0:T(8,128)} %get-tuple-element.4) | data formatting | bytes 16384
  36.6 1.3 %copy.12 = f32[16,128]{1,0:T(8,128)} copy(f32[16,128]{1,0:T(8,128)} %get-tuple-element.5) | data formatting | bytes 16384

commit v3 on v2

--- a/solution.py
+++ b/solution.py
@@ -11,8 +11,6 @@
 
 
 def partner(me, m, n):
-    if n & (n - 1):
-        return lax.rem(me + m, n)
     other, digit = me, 1
     while digit < n:
         if m & digit:
@@ -38,8 +36,7 @@
     kept_ref,
     dec_ref,
     enc_ref,
-    edges_ref,
-    weights_ref,
+    both_ref,
     ids_ref,
     layers_ref,
     acts_ref,
@@ -48,7 +45,8 @@
     meta_out,
     meta_in,
     rows_out,
-    rows_in,
+    near_in,
+    far_in,
     part_out,
     part_in,
     total_out,
@@ -62,8 +60,12 @@
     stored, width = dec_ref.shape
     feats = n * mine
     cap = 2 * mine
-    chunk = width // n
+    half = n // 2
+    spot = lax.rem(me, half)
+    chunk = width // half
     offsets = far_first(n)
+    across = [m for m in offsets if m >= half]
+    within = [m for m in offsets if m < half]
 
     loads = [
         pltpu.make_async_copy(dec_ref, stored_vm.at[pl.ds(0, stored)], load_sem.at[0]),
@@ -101,9 +103,9 @@
 
     pl.semaphore_wait(barrier, n - 1)
 
-    def exchange(phase, source, target):
+    def exchange(phase, partners, source, target):
         copies = []
-        for m in offsets:
+        for m in partners:
             copy = pltpu.make_async_remote_copy(
                 src_ref=source(partner(me, m, n)),
                 dst_ref=target,
@@ -116,7 +118,7 @@
             copies.append(copy)
         return copies
 
-    first = exchange(0, lambda p: meta_out, meta_in.at[me])
+    first = exchange(0, offsets, lambda peer: meta_out, meta_in.at[me])
     before = (iota((feats, feats), 0) < iota((feats, feats), 1)).astype(jnp.bfloat16)
     for copy in first:
         copy.wait_recv()
@@ -154,19 +156,21 @@
             preferred_element_type=jnp.float32,
         ).astype(jnp.bfloat16)
 
-    def take_and_give(p):
+    def far_rows(peer):
+        p = lax.rem(peer, half)
         rows_out[p] = selected(p)
-        return rows_out.at[p]
-
-    bulk = exchange(1, take_and_give, rows_in.at[me])
-    rows_in[me] = selected(me)
+        return rows_out.at[p, pl.ds(cap, cap)]
+
+    bulk = exchange(1, across, far_rows, far_in.at[spot])
+    bulk += exchange(1, within, lambda peer: rows_out.at[lax.rem(peer, half)], near_in.at[spot])
+    near_in[spot] = rows_out[spot]
 
     column_tiles, tiles = kept_ref.shape
     kept = jnp.transpose(kept_ref[...])
     spread = jnp.zeros((tiles, feats), jnp.int32)
     for c in range(column_tiles):
-        within = iota((tiles, feats), 1) // (feats // column_tiles) == c
-        spread = jnp.where(within, jnp.broadcast_to(kept[:, c : c + 1], (tiles, feats)), spread)
+        inside = iota((tiles, feats), 1) // (feats // column_tiles) == c
+        spread = jnp.where(inside, jnp.broadcast_to(kept[:, c : c + 1], (tiles, feats)), spread)
     spread = jnp.broadcast_to(spread[:, None, :], (tiles, mine, feats)).reshape(feats, feats)
     layer_down = jnp.transpose(jnp.broadcast_to(layer, (feats, feats)))
     allowed = jnp.where(
@@ -182,7 +186,8 @@
         preferred_element_type=jnp.float32,
     )
     act_mine = jnp.sum(chosen_f * act, axis=1, keepdims=True)
-    place_of = owner * cap + place
+    away = jnp.where(owner // half == me // half, 0, half)
+    place_of = (away + owner % half) * cap + place
     position = (
         jnp.broadcast_to(place_of, (n * cap, feats)) == iota((n * cap, feats), 0)
     ).astype(jnp.float32)
@@ -190,29 +195,38 @@
 
     for copy in bulk:
         copy.wait_recv()
-    sources = rows_in[:, :cap, :].reshape(n * cap, chunk)
-    targets = rows_in[:, cap:, :].reshape(n * cap, chunk)
-    targets = jnp.dot(ordering, targets, preferred_element_type=jnp.float32).astype(jnp.bfloat16)
+    sources = near_in[:, :cap, :].reshape(half * cap, chunk)
+    targets = jnp.dot(
+        ordering[:, : half * cap],
+        near_in[:, cap:, :].reshape(half * cap, chunk),
+        preferred_element_type=jnp.float32,
+    )
+    targets += jnp.dot(
+        ordering[:, half * cap :],
+        far_in[...].reshape(half * cap, chunk),
+        preferred_element_type=jnp.float32,
+    )
+    targets = targets.astype(jnp.bfloat16)
     part = lax.dot_general(
         sources, targets, (((1,), (1,)), ((), ())), preferred_element_type=jnp.float32
     )
-    part_out[...] = part.reshape(n, cap, feats)
-    sums = exchange(2, lambda p: part_out.at[p], part_in.at[me])
-    part_in[me] = part_out[me]
+    part_out[...] = part.reshape(half, cap, feats)
+    sums = exchange(2, within, lambda peer: part_out.at[lax.rem(peer, half)], part_in.at[spot])
+    part_in[spot] = part_out[spot]
     for copy in sums:
         copy.wait_recv()
     dots = jnp.sum(part_in[...], axis=0)
     edges = jnp.where(allowed_mine > 0.0, act_mine * dots, 0.0)
-    edges_ref[...] = edges
+    both_ref[0] = edges
     magnitude = jnp.abs(edges)
     partial = jnp.sum(magnitude.reshape(cap // 8, 8, feats), axis=0)
     total_out[...] = partial
     total_in[me] = partial
-    totals = exchange(3, lambda p: total_out, total_in.at[me])
+    totals = exchange(3, offsets, lambda peer: total_out, total_in.at[me])
     for copy in totals:
         copy.wait_recv()
     total = jnp.sum(jnp.sum(total_in[...], axis=0), axis=0, keepdims=True)
-    weights_ref[...] = magnitude * jnp.maximum(count, 1.0) / jnp.maximum(total, 1.0)
+    both_ref[1] = magnitude * jnp.maximum(count, 1.0) / jnp.maximum(total, 1.0)
     for copy in first + bulk + sums + totals:
         copy.wait_send()
 
@@ -223,15 +237,16 @@
     def shards(ids, layers, acts, kept, owner_map, decoder, encoder):
         mine = ids.shape[0]
         stored, width = decoder.shape
-        feats, cap = n * mine, 2 * mine
+        feats, cap, half = n * mine, 2 * mine, n // 2
+        chunk = width // half
         vmem = pl.BlockSpec(memory_space=pltpu.VMEM)
         hbm = pl.BlockSpec(memory_space=pltpu.HBM)
         result = jax.ShapeDtypeStruct((cap, feats), jnp.float32)
-        return pl.pallas_call(
+        both = pl.pallas_call(
             functools.partial(kernel, n),
-            out_shape=(result, result),
+            out_shape=jax.ShapeDtypeStruct((2, cap, feats), jnp.float32),
             in_specs=[hbm, hbm, hbm, hbm, vmem, hbm, hbm],
-            out_specs=(vmem, vmem),
+            out_specs=vmem,
             scratch_shapes=[
                 pltpu.SMEM(ids.shape, jnp.int32),
                 pltpu.SMEM(layers.shape, jnp.int32),
@@ -240,10 +255,11 @@
                 pltpu.VMEM((2 * stored, width), decoder.dtype),
                 pltpu.VMEM((8, feats), jnp.float32),
                 pltpu.VMEM((n, 8, feats), jnp.float32),
-                pltpu.VMEM((n, 2 * cap, width // n), decoder.dtype),
-                pltpu.VMEM((n, 2 * cap, width // n), decoder.dtype),
-                pltpu.VMEM((n, cap, feats), jnp.float32),
-                pltpu.VMEM((n, cap, feats), jnp.float32),
+                pltpu.VMEM((half, 2 * cap, chunk), decoder.dtype),
+                pltpu.VMEM((half, 2 * cap, chunk), decoder.dtype),
+                pltpu.VMEM((half, cap, chunk), decoder.dtype),
+                pltpu.VMEM((half, cap, feats), jnp.float32),
+                pltpu.VMEM((half, cap, feats), jnp.float32),
                 pltpu.VMEM((8, feats), jnp.float32),
                 pltpu.VMEM((n, 8, feats), jnp.float32),
                 pltpu.SemaphoreType.DMA((6,)),
@@ -254,6 +270,7 @@
                 collective_id=0, has_side_effects=True, vmem_limit_bytes=64 * 1024 * 1024
             ),
         )(ids, layers, acts, owner_map, kept.T, decoder, encoder)
+        return both[0], both[1]
 
     split = P(("groups", "row"))
     wide = P(("groups", "row"), None)

time: 38.2 us -> 36.5 us (0.955)
  local copies, waits for them, and re-layouts: 2.59 us -> 1.32 us
    unnamed x2 -> x0, local copies, waits for them, and re-layouts: 2.59 us -> none
    squeeze x0 -> x1, local copies, waits for them, and re-layouts: none -> 1.32 us  [shards(): return (both[0], both[1])]
where the time goes in v3:
time: 36.5 us; the launch traced here: 36.3 us
  Pallas kernels  34.3 us (94%)
  local copies, waits for them, and re-layouts  1.32 us (4%)
  between operations  0.64 us (2%)
    pallas_call x1, Pallas kernels, shards(): pl.pallas_call(functools.partial(kernel, n), out_shape=jax.ShapeDtypeStru...  34.3 us
    squeeze x1, local copies, waits for them, and re-layouts, shards(): return (both[0], both[1])  1.32 us

profile of v3, /device:TPU:0, one launch (start us, length us, event | category | flops | bytes accessed | tf_op | source)
XLA Modules:
  0.0 36.3 jit_solution(6445110876457026945)
XLA Ops:
  0.6 34.3 %shard_map.86 = f32[2,16,128]{2,1,0:T(8,128)} custom-call(s32[8]{0:T(128)} %ids_hbm.1, s32[8]{0:T(128)} %layers_hbm.1, f32[8]{0:T(128)} %acts_hbm.1, s32[2048]{0:T(1024)} %map_hbm.1, s32[4,16]{1,0:T(4,128)} %bitcast.5, bf16[128,8192]{1,0:T(8,128)(2,1)} %dec_ref.1, bf16[128,8192]{1,0:T(8,128)(2,1)} %enc_ref.1), custom_call_target="tpu_custom_call" | custom-call | tf_op jit(solution)/shard_map/pallas_call | solution.py:245
  34.9 1.3 %slice_bitcast_fusion = (f32[16,128]{1,0:T(8,128)}, f32[16,128]{1,0:T(8,128)}) fusion(f32[2,16,128]{2,1,0:T(8,128)} %shard_map.86), kind=kLoop, calls=%fused_computation | loop fusion | bytes 32768 | tf_op jit(solution)/shard_map/squeeze | solution.py:273

commit v4 on v3

--- a/solution.py
+++ b/solution.py
@@ -86,9 +86,9 @@
             barrier, inc=1, device_id={"row": partner(me, m, n)}, device_id_type=MESH
         )
 
-    lane = iota((8, feats), 1)
-    field = iota((8, feats), 0)
-    block = jnp.zeros((8, feats), jnp.float32)
+    lane = iota((4, feats), 1)
+    field = iota((4, feats), 0)
+    block = jnp.zeros((4, feats), jnp.float32)
     for load in small:
         load.wait()
     for k in range(mine):
@@ -219,13 +219,13 @@
     edges = jnp.where(allowed_mine > 0.0, act_mine * dots, 0.0)
     both_ref[0] = edges
     magnitude = jnp.abs(edges)
-    partial = jnp.sum(magnitude.reshape(cap // 8, 8, feats), axis=0)
+    partial = jnp.sum(magnitude, axis=0, keepdims=True)
     total_out[...] = partial
     total_in[me] = partial
     totals = exchange(3, offsets, lambda peer: total_out, total_in.at[me])
     for copy in totals:
         copy.wait_recv()
-    total = jnp.sum(jnp.sum(total_in[...], axis=0), axis=0, keepdims=True)
+    total = jnp.sum(total_in[...], axis=0)
     both_ref[1] = magnitude * jnp.maximum(count, 1.0) / jnp.maximum(total, 1.0)
     for copy in first + bulk + sums + totals:
         copy.wait_send()
@@ -241,10 +241,9 @@
         chunk = width // half
         vmem = pl.BlockSpec(memory_space=pltpu.VMEM)
         hbm = pl.BlockSpec(memory_space=pltpu.HBM)
-        result = jax.ShapeDtypeStruct((cap, feats), jnp.float32)
         both = pl.pallas_call(
             functools.partial(kernel, n),
-            out_shape=jax.ShapeDtypeStruct((2, cap, feats), jnp.float32),
+            out_shape=pltpu.VMEM((2, cap, feats), jnp.float32),
             in_specs=[hbm, hbm, hbm, hbm, vmem, hbm, hbm],
             out_specs=vmem,
             scratch_shapes=[
@@ -253,21 +252,21 @@
                 pltpu.SMEM(acts.shape, jnp.float32),
                 pltpu.SMEM(owner_map.shape, jnp.int32),
                 pltpu.VMEM((2 * stored, width), decoder.dtype),
-                pltpu.VMEM((8, feats), jnp.float32),
-                pltpu.VMEM((n, 8, feats), jnp.float32),
+                pltpu.VMEM((4, feats), jnp.float32),
+                pltpu.VMEM((n, 4, feats), jnp.float32),
                 pltpu.VMEM((half, 2 * cap, chunk), decoder.dtype),
                 pltpu.VMEM((half, 2 * cap, chunk), decoder.dtype),
                 pltpu.VMEM((half, cap, chunk), decoder.dtype),
                 pltpu.VMEM((half, cap, feats), jnp.float32),
                 pltpu.VMEM((half, cap, feats), jnp.float32),
-                pltpu.VMEM((8, feats), jnp.float32),
-                pltpu.VMEM((n, 8, feats), jnp.float32),
+                pltpu.VMEM((1, feats), jnp.float32),
+                pltpu.VMEM((n, 1, feats), jnp.float32),
                 pltpu.SemaphoreType.DMA((6,)),
                 pltpu.SemaphoreType.DMA((4, n)),
                 pltpu.SemaphoreType.DMA((4, n)),
             ],
             compiler_params=pltpu.CompilerParams(
-                collective_id=0, has_side_effects=True, vmem_limit_bytes=64 * 1024 * 1024
+                collective_id=0, has_side_effects=True, vmem_limit_bytes=56 * 1024 * 1024
             ),
         )(ids, layers, acts, owner_map, kept.T, decoder, encoder)
         return both[0], both[1]

time: 36.5 us -> 34.7 us (0.951)
  Pallas kernels: 34.3 us -> 33.2 us
  local copies, waits for them, and re-layouts: 1.32 us -> 0.61 us
    pallas_call x1, Pallas kernels: 34.3 us -> 33.2 us  [shards(): pl.pallas_call(functools.partial(kernel, n), out_shape=pltpu.VMEM((2, cap...]
    squeeze x1, local copies, waits for them, and re-layouts: 1.32 us -> 0.61 us  [shards(): return (both[0], both[1])]
where the time goes in v4:
time: 34.7 us; the launch traced here: 34.5 us
  Pallas kernels  33.2 us (96%)
  between operations  0.64 us (2%)
  local copies, waits for them, and re-layouts  0.61 us (2%)
    pallas_call x1, Pallas kernels, shards(): pl.pallas_call(functools.partial(kernel, n), out_shape=pltpu.VMEM((2, cap...  33.2 us

profile of v4, /device:TPU:0, one launch (start us, length us, event | category | flops | bytes accessed | tf_op | source)
XLA Modules:
  0.0 34.5 jit_solution(11380624876106363552)
XLA Ops:
  0.6 33.2 %shard_map.86 = f32[2,16,128]{2,1,0:T(8,128)S(1)} custom-call(s32[8]{0:T(128)} %ids_hbm.1, s32[8]{0:T(128)} %layers_hbm.1, f32[8]{0:T(128)} %acts_hbm.1, s32[2048]{0:T(1024)} %map_hbm.1, s32[4,16]{1,0:T(4,128)} %bitcast.5, bf16[128,8192]{1,0:T(8,128)(2,1)} %dec_ref.1, bf16[128,8192]{1,0:T(8,128)(2,1)} %enc_ref.1), custom_call_target="tpu_custom_call" | custom-call | tf_op jit(solution)/shard_map/pallas_call | solution.py:244
  33.9 0.6 %slice_bitcast_fusion = (f32[16,128]{1,0:T(8,128)}, f32[16,128]{1,0:T(8,128)}) fusion(f32[2,16,128]{2,1,0:T(8,128)S(1)} %shard_map.86), kind=kLoop, calls=%fused_computation | loop fusion | bytes 32768 | tf_op jit(solution)/shard_map/squeeze | solution.py:272
